TPU v7x, 32 devices: a whole 2x2x4 slice. The times are simulated.
32 devices in a mesh: dp: 8 (over y, x, core), ctx: 4 (over z).
Axes of the slice: x: 2, y: 2, z: 4, core: 2. Of those that a mesh axis runs over, the one named last changes fastest.
Arguments:
- queries: bfloat16 [8, 4096, 512], P('dp', 'ctx'), may hold values from -6 to 6
- keys: bfloat16 [8, 4096, 128], P('dp', 'ctx'), may hold values from -6 to 6
- values: bfloat16 [8, 4096, 128], P('dp', 'ctx'), may hold values from -6 to 6
- dest_replica: int32 [8, 64], P('dp', 'ctx'), may hold values from 0 to 7, as said below
- dest_slot: int32 [8, 64], P('dp', 'ctx'), may hold values from 0 to 63, as said below
- doc_lengths: int32 [8, 16], P('dp'), may hold values from 1 to 32, 64 in all within a row
- tile_mask: int32 [8, 64, 64], P('dp', 'ctx'), may hold values 0 or 1
Outputs:
- attended: bfloat16 [8, 4096, 512], P('dp', 'ctx')
Inputs may be any that keep to these rules, and one draw needn't show every extreme that they name: `dest_replica`: every block of a pack receives exactly one arriving block; a block keeps its shard along ctx (dest_slot // 16 equals the arriving block's own b // 16); the 16 blocks of one device go to every pack, 2 to each. `dest_slot`: see dest_replica. `doc_lengths`: they sum to 64 in every pack, and the largest is 32 in every pack.
All inputs are finite; a program needn't handle non-finite values. No bound on the sum of `tile_mask` on one device may be relied on, other than what follows from the above.
Results may differ from a plain program's by a relative error of at most 0.0033.
Values may be sent and summed in bfloat16 or wider, within the bound.
No kernel may reach another device: no remote copies, remote signals or barrier semaphores. Data moves between devices by JAX's collectives and lax.ppermute only.
A program may use at most 64 MiB of HBM per device.

v0:
```python
import functools

import jax
import jax.numpy as jnp
from jax import lax
from jax.experimental import pallas as pl
from jax.experimental.pallas import tpu as pltpu
from jax.sharding import PartitionSpec as P

HEAD_WIDTH = 128
QUERY_HEADS = 4
SCALE = HEAD_WIDTH ** (-0.5)
NEVER = -1e30
FLOOR = -5e29
SLOT_ROWS = 16
VMEM_LIMIT = 32 * 1024 * 1024
VMEM_SMALL = 8 * 1024 * 1024

ANY = pl.BlockSpec(memory_space=pl.ANY)
SMEM = pl.BlockSpec(memory_space=pltpu.SMEM)
VMEM = pl.BlockSpec(memory_space=pltpu.VMEM)


def shifted(value, axis):
    count = lax.axis_size(axis)
    return lax.ppermute(value, axis, [(source, source + 1) for source in range(count - 1)])


def pack_kv_kernel(cap, targets, slots, keys_in, values_in, send_out,
                   keys, values, send, counts, slot_of, sem):
    packs = send.shape[0]
    blocks = targets.shape[1]
    size = keys.shape[1] // blocks
    half = cap * size
    loads = [
        pltpu.make_async_copy(keys_in, keys, sem.at[0]),
        pltpu.make_async_copy(values_in, values, sem.at[1]),
    ]
    for load in loads:
        load.start()
    for t in range(packs):
        counts[t] = 0
    places = []
    for j in range(blocks):
        t = targets[0, j]
        rank = counts[t]
        counts[t] = rank + 1
        slot_of[t * cap + rank] = lax.rem(slots[0, j], blocks)
        places.append((t, pl.multiple_of(rank * size, size)))
    row = lax.broadcasted_iota(jnp.int32, (SLOT_ROWS, HEAD_WIDTH), 0)
    for t in range(packs):
        listed = jnp.zeros(row.shape, jnp.int32)
        for i in range(cap):
            listed = jnp.where(row == i, slot_of[t * cap + i], listed)
        send[t, 2 * half:, :] = listed.astype(jnp.float32).astype(jnp.bfloat16)
    for load, held, shift in zip(loads, (keys, values), (0, half)):
        load.wait()
        for j, (t, to) in enumerate(places):
            send[t, pl.ds(to + shift, size), :] = held[0, j * size:(j + 1) * size, :]
    store = pltpu.make_async_copy(send, send_out, sem.at[2])
    store.start()
    store.wait()


def pack_q_kernel(cap, targets, queries, send, counts):
    packs = send.shape[0]
    blocks = targets.shape[1]
    size = queries.shape[1] // blocks
    for t in range(packs):
        counts[t] = 0
    for j in range(blocks):
        t = targets[0, j]
        rank = counts[t]
        counts[t] = rank + 1
        to = pl.multiple_of(rank * size, size)
        send[t, pl.ds(to, size), :] = queries[0, j * size:(j + 1) * size, :]


def place_kernel(cap, received, placed, order):
    packs = received.shape[0]
    size = placed.shape[1] // (packs * cap)
    half = cap * size
    for s in range(packs):
        listed = received[s, 2 * half:, :].astype(jnp.float32).astype(jnp.int32)
        for i in range(cap):
            slot = listed[i, 0]
            order[0, slot] = s * cap + i
            rows = pl.ds(pl.multiple_of(slot * size, size), size)
            placed[0, rows, :] = received[s, i * size:(i + 1) * size, :]
            placed[1, rows, :] = received[s, half + i * size:half + (i + 1) * size, :]


def first_document(lengths, position):
    start, end = jnp.int32(0), jnp.int32(0)
    total = jnp.int32(0)
    for j in range(lengths.shape[1]):
        after = total + lengths[0, j]
        inside = (total <= position) & (position < after)
        start = jnp.where(inside, total, start)
        end = jnp.where(inside, after, end)
        total = after
    return start, end


def reach_of(lengths, place, offset, blocks):
    start, end = first_document(lengths, place * blocks)
    low = (place - offset) * blocks
    rows = jnp.where(start < low + blocks, jnp.minimum(end - place * blocks, blocks), 0)
    return jnp.where(low >= 0, rows, 0), jnp.maximum(start - low, 0)


def prepare(keys, values, bias, kv, lengths, tiles, place, offset):
    blocks = bias.shape[0]
    tokens = kv.shape[1]
    size = tokens // blocks
    block = lax.broadcasted_iota(jnp.int32, (tokens, HEAD_WIDTH), 1)
    of_key = lax.broadcasted_iota(jnp.int32, (tokens, HEAD_WIDTH), 0) // size
    keys[:, :HEAD_WIDTH] = kv[0]
    keys[:, HEAD_WIDTH:] = (block == of_key).astype(jnp.float32).astype(jnp.bfloat16)
    values[:, :HEAD_WIDTH] = kv[1]
    values[:, HEAD_WIDTH:] = jnp.ones((tokens, HEAD_WIDTH), jnp.bfloat16)

    low = (place - offset) * blocks
    key_block = low + lax.broadcasted_iota(jnp.int32, (1, HEAD_WIDTH), 1)
    query_block = place * blocks + lax.broadcasted_iota(jnp.int32, (blocks, 1), 0)
    key_doc = jnp.zeros((1, HEAD_WIDTH), jnp.int32)
    query_doc = jnp.zeros((blocks, 1), jnp.int32)
    end = jnp.int32(0)
    for j in range(lengths.shape[1]):
        end = end + lengths[0, j]
        key_doc = key_doc + (key_block >= end).astype(jnp.int32)
        query_doc = query_doc + (query_block >= end).astype(jnp.int32)
    spread = lax.broadcasted_iota(jnp.int32, (tiles.shape[2], HEAD_WIDTH), 0) == key_block
    listed = jnp.dot(
        tiles[0].astype(jnp.float32).astype(jnp.bfloat16),
        spread.astype(jnp.float32).astype(jnp.bfloat16),
        preferred_element_type=jnp.float32,
    )
    allowed = (query_doc == key_doc) & (key_block <= query_block) & (key_block >= 0)
    allowed = allowed & ((listed > 0.5) | (key_block == query_block))
    bias[...] = jnp.where(allowed, 0.0, NEVER)


def score(received, order, bias, i, keys, size):
    source = pl.ds(pl.multiple_of(order[0, i] * size, size), size)
    barred = jnp.broadcast_to(bias[pl.ds(i, 1), :], (QUERY_HEADS * size, HEAD_WIDTH))
    rows = jnp.concatenate(
        [heads_as_rows(received[source, :]), barred.astype(jnp.bfloat16)], axis=1
    )
    return lax.dot_general(
        rows, keys, (((1,), (1,)), ((), ())), preferred_element_type=jnp.float32
    )


def heads_as_rows(block):
    return jnp.concatenate(
        [block[:, h * HEAD_WIDTH:(h + 1) * HEAD_WIDTH] for h in range(QUERY_HEADS)], axis=0
    )


def heads_as_columns(rows, size):
    return jnp.concatenate(
        [rows[h * size:(h + 1) * size] for h in range(QUERY_HEADS)], axis=1
    )


def own_kernel(
    order, lengths, tiles, received, kv,
    out, state_o, state_l,
    keys, values, bias, stage, sem,
):
    place = lax.axis_index("ctx")
    blocks = bias.shape[0]
    tokens = kv.shape[1]
    size = tokens // blocks
    group = QUERY_HEADS * size
    prepare(keys, values, bias, kv, lengths, tiles, place, 0)
    row = lax.rem(lax.broadcasted_iota(jnp.int32, (group, 2 * size), 0), size)
    lane = lax.broadcasted_iota(jnp.int32, (group, 2 * size), 1)

    def start(i):
        return score(received, order, bias, i, keys[:(i // 2 + 1) * 2 * size, :], size)

    copies = []
    scores = start(0)
    for i in range(blocks):
        ahead = start(i + 1) if i + 1 < blocks else None
        rows = slice(i * size, (i + 1) * size)
        span = slice(i * group, (i + 1) * group)
        width = scores.shape[1]
        edge = width - 2 * size
        tail = jnp.where(lane - (i % 2) * size > row, NEVER, scores[:, edge:])
        scores = jnp.concatenate([scores[:, :edge], tail], axis=1) if edge else tail
        top = jnp.max(scores, axis=1, keepdims=True) * SCALE
        weights = jnp.exp(scores * SCALE - top).astype(jnp.bfloat16)
        sums = jnp.dot(weights, values[:width, :], preferred_element_type=jnp.float32)
        denominator = sums[:, HEAD_WIDTH:]
        result = sums[:, :HEAD_WIDTH] / denominator
        stage[rows, :] = heads_as_columns(result, size).astype(jnp.bfloat16)
        state_o[span, :] = result
        state_l[span, :] = top + jnp.log(denominator)
        copy = pltpu.make_async_copy(stage.at[rows], out.at[0, rows], sem.at[i])
        copy.start()
        copies.append(copy)
        scores = ahead
    for copy in copies:
        copy.wait()


def hop_kernel(
    offset, order, lengths, tiles, received, kv, out_in, state_o_in, state_l_in,
    out, state_o, state_l,
    keys, values, bias, stage, sem,
):
    place = lax.axis_index("ctx")
    blocks = bias.shape[0]
    tokens = kv.shape[1]
    size = tokens // blocks
    group = QUERY_HEADS * size
    reads, first = reach_of(lengths, place, offset, blocks)

    @pl.when(reads > 0)
    def _():
        prepare(keys, values, bias, kv, lengths, tiles, place, offset)

        def over(low, together):
            def start(i):
                return score(received, order, bias, i, keys[low:, :], size)

            def end(i, scores):
                span = pl.ds(pl.multiple_of(i * group, group), group)
                top = jnp.maximum(jnp.max(scores, axis=1, keepdims=True), FLOOR) * SCALE
                weights = jnp.exp(scores * SCALE - top).astype(jnp.bfloat16)
                sums = jnp.dot(weights, values[low:, :], preferred_element_type=jnp.float32)
                before = state_l_in[span, :]
                most = jnp.maximum(before, top)
                old = jnp.exp(before - most)
                new = jnp.exp(top - most)
                denominator = old + new * sums[:, HEAD_WIDTH:]
                result = (
                    old * state_o_in[span, :] + new * sums[:, :HEAD_WIDTH]
                ) / denominator
                rows = pl.ds(pl.multiple_of(i * size, size), size)
                stage[rows, :] = heads_as_columns(result, size).astype(jnp.bfloat16)
                if offset == 1:
                    state_o[span, :] = result
                    state_l[span, :] = most + jnp.log(denominator)

            def step(n, carry):
                i = n * together
                scores = start(i)
                for u in range(together):
                    ahead = start(i + u + 1) if u + 1 < together else None
                    end(i + u, scores)
                    scores = ahead
                rows = pl.ds(pl.multiple_of(i * size, size), together * size)
                pltpu.make_async_copy(stage.at[rows], out.at[0, rows], sem).start()
                return carry

            def finish(n, carry):
                rows = pl.ds(pl.multiple_of(n * together * size, size), together * size)
                pltpu.make_async_copy(stage.at[rows], out.at[0, rows], sem).wait()
                return carry

            steps = pl.cdiv(reads, together)
            lax.fori_loop(0, steps, step, 0)
            lax.fori_loop(0, steps, finish, 0)

        part = first // (blocks // 4)
        for n, together in enumerate((4, 4, 4, 4)):
            pl.when(part == n)(functools.partial(over, n * (tokens // 4), together))


def per_device(queries, keys, values, dest_replica, dest_slot, doc_lengths, tile_mask):
    tokens = queries.shape[1]
    width = queries.shape[2]
    blocks = dest_replica.shape[1]
    size = tokens // blocks
    packs = lax.axis_size("dp")
    cap = blocks // packs
    bf16, f32 = jnp.bfloat16, jnp.float32
    rows = tokens * QUERY_HEADS
    params = pltpu.CompilerParams(vmem_limit_bytes=VMEM_LIMIT)
    small = pltpu.CompilerParams(vmem_limit_bytes=VMEM_SMALL)

    def cost(flops, moved):
        return pl.CostEstimate(flops=flops, bytes_accessed=moved, transcendentals=0)

    def route(sent):
        return lax.all_to_all(sent, "dp", split_axis=0, concat_axis=0, tiled=True)

    dma = pltpu.SemaphoreType.DMA
    counts = pltpu.SMEM((packs,), jnp.int32)
    kv_send = pl.pallas_call(
        functools.partial(pack_kv_kernel, cap),
        out_shape=jax.ShapeDtypeStruct((packs, 2 * cap * size + SLOT_ROWS, HEAD_WIDTH), bf16),
        in_specs=[SMEM, SMEM, ANY, ANY],
        out_specs=ANY,
        scratch_shapes=[
            pltpu.VMEM(keys.shape, bf16),
            pltpu.VMEM(values.shape, bf16),
            pltpu.VMEM((packs, 2 * cap * size + SLOT_ROWS, HEAD_WIDTH), bf16),
            counts,
            pltpu.SMEM((blocks,), jnp.int32),
            dma((3,)),
        ],
        cost_estimate=cost(0, 4 * tokens * HEAD_WIDTH * 2),
        name="pack_kv",
    )(dest_replica, dest_slot, keys, values)
    kv_recv = route(kv_send)
    q_send = pl.pallas_call(
        functools.partial(pack_q_kernel, cap),
        out_shape=jax.ShapeDtypeStruct((packs, cap * size, width), bf16),
        in_specs=[SMEM, VMEM],
        out_specs=VMEM,
        scratch_shapes=[counts],
        compiler_params=small,
        cost_estimate=cost(0, 2 * tokens * width * 2),
        name="pack_q",
    )(dest_replica, queries)
    kv, order = pl.pallas_call(
        functools.partial(place_kernel, cap),
        out_shape=(
            jax.ShapeDtypeStruct((2, tokens, HEAD_WIDTH), bf16),
            jax.ShapeDtypeStruct((1, blocks), jnp.int32),
        ),
        in_specs=[VMEM],
        out_specs=(VMEM, SMEM),
        compiler_params=small,
        cost_estimate=cost(0, 4 * tokens * HEAD_WIDTH * 2),
        name="place_kv",
    )(kv_recv)

    q_send, kv = lax.optimization_barrier((q_send, kv))
    q_recv = route(q_send).reshape(tokens, width)

    state_shapes = (
        jax.ShapeDtypeStruct((1, tokens, width), bf16),
        jax.ShapeDtypeStruct((rows, HEAD_WIDTH), f32),
        jax.ShapeDtypeStruct((rows, HEAD_WIDTH), f32),
    )
    operands = [
        pltpu.VMEM((tokens, 2 * HEAD_WIDTH), bf16),
        pltpu.VMEM((tokens, 2 * HEAD_WIDTH), bf16),
        pltpu.VMEM((blocks, HEAD_WIDTH), f32),
    ]
    stage = pltpu.VMEM((tokens, width), bf16)
    state = pl.pallas_call(
        own_kernel,
        out_shape=state_shapes,
        in_specs=[SMEM, SMEM, VMEM, VMEM, VMEM],
        out_specs=(ANY, VMEM, VMEM),
        scratch_shapes=operands + [stage, dma((blocks,))],
        compiler_params=params,
        cost_estimate=cost(2 * 2 * rows * tokens * HEAD_WIDTH, 8 * tokens * width),
        name="attend_own",
    )(order, doc_lengths, tile_mask, q_recv, kv)
    later = kv
    for offset in (1, 2):
        kv = shifted(later, "ctx")
        if offset == 1:
            later, *state = lax.optimization_barrier((kv, *state))
        state = pl.pallas_call(
            functools.partial(hop_kernel, offset),
            out_shape=state_shapes,
            in_specs=[SMEM, SMEM, VMEM, VMEM, VMEM, ANY, VMEM, VMEM],
            out_specs=(ANY, VMEM, VMEM),
            scratch_shapes=operands + [stage, dma],
            input_output_aliases={5: 0, 6: 1, 7: 2},
            compiler_params=params,
            cost_estimate=cost(2 * 2 * rows * tokens * HEAD_WIDTH, 8 * tokens * width),
            name=f"attend_back_{offset}",
        )(order, doc_lengths, tile_mask, q_recv, kv, *state)
    return state[0]


def solution(mesh):
    return jax.shard_map(
        per_device,
        mesh=mesh,
        in_specs=(
            P("dp", "ctx", None),
            P("dp", "ctx", None),
            P("dp", "ctx", None),
            P("dp", "ctx"),
            P("dp", "ctx"),
            P("dp", None),
            P("dp", "ctx", None),
        ),
        out_specs=P("dp", "ctx", None),
        check_vma=False,
    )
```

profile of v0, /device:TPU:27, one launch (start us, length us, event | category | flops | bytes accessed | tf_op | source)
XLA Modules:
  0.0 60.6 jit_solution(8024832249796110285)
XLA Ops:
  0.0 0.0 copy-start.1
  0.0 0.0 copy-start
  0.0 2.7 %pack_kv.1 = bf16[8,272,128]{2,1,0:T(8,128)(2,1)} custom-call(s32[1,16]{1,0:T(1,128)} %targets.3, s32[1,16]{1,0:T(1,128)} %slots.1, bf16[1,1024,128]{2,1,0:T(8,128)(2,1)} %keys_in.1, bf16[1,1024,128]{2,1,0:T(8,128)(2,1)} %values_in.1), custom_call_target="tpu_custom_call" | custom-call | bytes 1048576 | tf_op jit(solution)/shard_map/pack_kv/pallas_call | solution.py:294
  2.7 4.6 %all-to-all-start = ((bf16[8,272,128]{2,1,0:T(8,128)(2,1)}), bf16[8,272,128]{2,1,0:T(8,128)(2,1)S(1)}, u32[]{:S(2)}, u32[]{:S(2)}) async-start(bf16[8,272,128]{2,1,0:T(8,128)(2,1)} %pack_kv.1), calls=%async_computation | async-start | bytes 1114112 | tf_op jit(solution)/shard_map/all_to_all | solution.py:290
  7.3 0.0 copy-done.1
  7.3 0.0 copy-done
  7.3 0.0 copy-start.2
  7.3 0.0 copy-start.3
  7.3 1.6 %pack_q.1 = bf16[8,128,512]{2,1,0:T(8,128)(2,1)} custom-call(s32[1,16]{1,0:T(1,128)S(1)} %copy-done.1, bf16[1,1024,512]{2,1,0:T(8,128)(2,1)S(1)} %copy-done), custom_call_target="tpu_custom_call" | custom-call | bytes 2097152 | tf_op jit(solution)/shard_map/pack_q/pallas_call | solution.py:311
  8.9 6.9 %all-to-all-done.received = bf16[8,272,128]{2,1,0:T(8,128)(2,1)S(1)} async-done(((bf16[8,272,128]{2,1,0:T(8,128)(2,1)}), bf16[8,272,128]{2,1,0:T(8,128)(2,1)S(1)}, u32[]{:S(2)}, u32[]{:S(2)}) %all-to-all-start) | async-done | bytes 557088 | tf_op jit(solution)/shard_map/all_to_all | solution.py:290
  15.8 0.7 %place_kv.1 = (bf16[2,1024,128]{2,1,0:T(8,128)(2,1)S(1)}, s32[1,16]{1,0:T(1,128)S(1)}) custom-call(bf16[8,272,128]{2,1,0:T(8,128)(2,1)S(1)} %all-to-all-done.received), custom_call_target="tpu_custom_call" | custom-call | bytes 1048576 | tf_op jit(solution)/shard_map/place_kv/pallas_call | solution.py:321
  16.5 5.0 %all-to-all-start.1 = ((bf16[8,128,512]{2,1,0:T(8,128)(2,1)}), bf16[8,128,512]{2,1,0:T(8,128)(2,1)S(1)}, u32[]{:S(2)}, u32[]{:S(2)}) async-start(bf16[8,128,512]{2,1,0:T(8,128)(2,1)} %pack_q.1), calls=%async_computation.1 | async-start | bytes 2097152 | tf_op jit(solution)/shard_map/all_to_all | solution.py:290
  21.5 1.3 %collective-permute-start = (bf16[2,1024,128]{2,1,0:T(8,128)(2,1)S(1)}, bf16[2,1024,128]{2,1,0:T(8,128)(2,1)S(1)}, u32[]{:S(2)}, u32[]{:S(2)}) collective-permute-start(bf16[2,1024,128]{2,1,0:T(8,128)(2,1)S(1)} %get-tuple-element.23.kv), channel_id=1, source_target_pairs={{0,1},{1,2},{2,3},{4,5},{5,6},{6,7},{8,9},{9,10},{10,11},{12,13},{... | collective-permute-start | bytes 1572872 | tf_op jit(solution)/shard_map/ppermute | solution.py:26
  22.8 12.5 %all-to-all-done.1 = bf16[8,128,512]{2,1,0:T(8,128)(2,1)S(1)} async-done(((bf16[8,128,512]{2,1,0:T(8,128)(2,1)}), bf16[8,128,512]{2,1,0:T(8,128)(2,1)S(1)}, u32[]{:S(2)}, u32[]{:S(2)}) %all-to-all-start.1) | async-done | bytes 1048608 | tf_op jit(solution)/shard_map/all_to_all | solution.py:290
  35.4 0.0 copy-done.2
  35.4 0.0 copy-done.3
  35.4 5.5 %attend_own.1 = (bf16[1,1024,512]{2,1,0:T(8,128)(2,1)}, f32[4096,128]{1,0:T(8,128)S(1)}, f32[4096,128]{1,0:T(8,128)S(1)}) custom-call(s32[1,16]{1,0:T(1,128)S(1)} %get-tuple-element.20.order, s32[1,16]{1,0:T(1,128)S(1)} %copy-done.3, s32[1,16,64]{2,1,0:T(8,128)S(1)} %copy-done.2, bf16[1024,512]{1,0:T(8,128)(2,1)S(1)} %bitcast.1, ...), custom_call_target="tpu_custom_call" | custom-call | flops 2147483648 | bytes 4194304 | tf_op jit(solution)/shard_map/attend_own/pallas_call | solution.py:348
  40.9 0.0 collective-permute-done.kv
  40.9 1.3 %collective-permute-start.1 = (bf16[2,1024,128]{2,1,0:T(8,128)(2,1)S(1)}, bf16[2,1024,128]{2,1,0:T(8,128)(2,1)S(1)}, u32[]{:S(2)}, u32[]{:S(2)}) collective-permute-start(bf16[2,1024,128]{2,1,0:T(8,128)(2,1)S(1)} %collective-permute-done.kv), channel_id=1, source_target_pairs={{0,1},{1,2},{2,3},{4,5},{5,6},{6,7},{8,9},{9,10},{10,11},{12,13},{... | collective-permute-start | bytes 1572872 | tf_op jit(solution)/shard_map/ppermute | solution.py:26
  42.2 5.1 %attend_back_1.1 = (bf16[1,1024,512]{2,1,0:T(8,128)(2,1)}, f32[4096,128]{1,0:T(8,128)S(1)}, f32[4096,128]{1,0:T(8,128)S(1)}) custom-call(s32[1,16]{1,0:T(1,128)S(1)} %get-tuple-element.20.order, s32[1,16]{1,0:T(1,128)S(1)} %copy-done.3, s32[1,16,64]{2,1,0:T(8,128)S(1)} %copy-done.2, ...), custom_call_target="tpu_custom_call", output_to_operand_aliasing={{0}: (5, {}), {1}: (6, {}), {2}: (7, {})} | custom-call | flops 2147483648 | bytes 4194304 | tf_op jit(solution)/shard_map/attend_back_1/pallas_call | solution.py:363
  47.3 8.6 %collective-permute-done.1.kv = bf16[2,1024,128]{2,1,0:T(8,128)(2,1)S(1)} collective-permute-done((bf16[2,1024,128]{2,1,0:T(8,128)(2,1)S(1)}, bf16[2,1024,128]{2,1,0:T(8,128)(2,1)S(1)}, u32[]{:S(2)}, u32[]{:S(2)}) %collective-permute-start.1) | collective-permute-done | bytes 524320 | tf_op jit(solution)/shard_map/ppermute | solution.py:26
  55.9 4.5 %attend_back_2.1 = (bf16[1,1024,512]{2,1,0:T(8,128)(2,1)}, f32[4096,128]{1,0:T(8,128)S(1)}, f32[4096,128]{1,0:T(8,128)S(1)}) custom-call(s32[1,16]{1,0:T(1,128)S(1)} %get-tuple-element.20.order, s32[1,16]{1,0:T(1,128)S(1)} %copy-done.3, s32[1,16,64]{2,1,0:T(8,128)S(1)} %copy-done.2, ...), custom_call_target="tpu_custom_call", output_to_operand_aliasing={{0}: (5, {}), {1}: (6, {}), {2}: (7, {})} | custom-call | flops 2147483648 | bytes 4194304 | tf_op jit(solution)/shard_map/attend_back_2/pallas_call | solution.py:363
Async XLA Ops:
  0.0 7.3 %copy-start.1 = (s32[1,16]{1,0:T(1,128)S(1)}, s32[1,16]{1,0:T(1,128)}, u32[]{:S(2)}) copy-start(s32[1,16]{1,0:T(1,128)} %targets.3) | copy-start | bytes 196
  0.0 7.3 %copy-start = (bf16[1,1024,512]{2,1,0:T(8,128)(2,1)S(1)}, bf16[1,1024,512]{2,1,0:T(8,128)(2,1)}, u32[]{:S(2)}) copy-start(bf16[1,1024,512]{2,1,0:T(8,128)(2,1)} %queries.1) | copy-start | bytes 3145732
  2.7 13.1 %all-to-all-start = ((bf16[8,272,128]{2,1,0:T(8,128)(2,1)}), bf16[8,272,128]{2,1,0:T(8,128)(2,1)S(1)}, u32[]{:S(2)}, u32[]{:S(2)}) async-start(bf16[8,272,128]{2,1,0:T(8,128)(2,1)} %pack_kv.1), calls=%async_computation | async-start | bytes 1114112 | tf_op jit(solution)/shard_map/all_to_all | solution.py:290
  7.3 28.1 %copy-start.2 = (s32[1,16,64]{2,1,0:T(8,128)S(1)}, s32[1,16,64]{2,1,0:T(8,128)}, u32[]{:S(2)}) copy-start(s32[1,16,64]{2,1,0:T(8,128)} %tiles.5) | copy-start | bytes 12292
  7.3 28.1 %copy-start.3 = (s32[1,16]{1,0:T(1,128)S(1)}, s32[1,16]{1,0:T(1,128)}, u32[]{:S(2)}) copy-start(s32[1,16]{1,0:T(1,128)} %lengths.5) | copy-start | bytes 196
  16.5 18.9 %all-to-all-start.1 = ((bf16[8,128,512]{2,1,0:T(8,128)(2,1)}), bf16[8,128,512]{2,1,0:T(8,128)(2,1)S(1)}, u32[]{:S(2)}, u32[]{:S(2)}) async-start(bf16[8,128,512]{2,1,0:T(8,128)(2,1)} %pack_q.1), calls=%async_computation.1 | async-start | bytes 2097152 | tf_op jit(solution)/shard_map/all_to_all | solution.py:290
  21.5 19.4 %collective-permute-start = (bf16[2,1024,128]{2,1,0:T(8,128)(2,1)S(1)}, bf16[2,1024,128]{2,1,0:T(8,128)(2,1)S(1)}, u32[]{:S(2)}, u32[]{:S(2)}) collective-permute-start(bf16[2,1024,128]{2,1,0:T(8,128)(2,1)S(1)} %get-tuple-element.23.kv), channel_id=1, source_target_pairs={{0,1},{1,2},{2,3},{4,5},{5,6},{6,7},{8,9},{9,10},{10,11},{12,13},{... | collective-permute-start | bytes 1572872 | tf_op jit(solution)/shard_map/ppermute | solution.py:26
  40.9 15.0 %collective-permute-start.1 = (bf16[2,1024,128]{2,1,0:T(8,128)(2,1)S(1)}, bf16[2,1024,128]{2,1,0:T(8,128)(2,1)S(1)}, u32[]{:S(2)}, u32[]{:S(2)}) collective-permute-start(bf16[2,1024,128]{2,1,0:T(8,128)(2,1)S(1)} %collective-permute-done.kv), channel_id=1, source_target_pairs={{0,1},{1,2},{2,3},{4,5},{5,6},{6,7},{8,9},{9,10},{10,11},{12,13},{... | collective-permute-start | bytes 1572872 | tf_op jit(solution)/shard_map/ppermute | solution.py:26
where the time goes:
time: 60.8 us; the launch traced here: 60.6 us
  waiting for transfers between devices  28 us (46%)
  Pallas kernels  20.1 us (33%)
  starting transfers between devices  12.2 us (20%)
    all_to_all x2, waiting for transfers between devices, route(): return lax.all_to_all(sent, 'dp', split_axis=0, concat_axis=0, tiled=True)  19.5 us
    pallas_call x2, Pallas kernels, per_device(): pl.pallas_call(functools.partial(hop_kernel, offset), out_shape=state_sha...  9.62 us
    all_to_all x2, starting transfers between devices, route(): return lax.all_to_all(sent, 'dp', split_axis=0, concat_axis=0, tiled=True)  9.61 us
    ppermute x2, waiting for transfers between devices, shifted(): lax.ppermute(value, axis, [(source, source + 1) for source in range(count...  8.57 us
    pallas_call x1, Pallas kernels, per_device(): pl.pallas_call(own_kernel, out_shape=state_shapes, in_specs=[SMEM, SMEM,...  5.53 us
    pallas_call x1, Pallas kernels, per_device(): pl.pallas_call(functools.partial(pack_kv_kernel, cap), out_shape=jax.Shap...  2.69 us
    ppermute x2, starting transfers between devices, shifted(): lax.ppermute(value, axis, [(source, source + 1) for source in range(count...  2.57 us
    pallas_call x1, Pallas kernels, per_device(): pl.pallas_call(functools.partial(pack_q_kernel, cap), out_shape=jax.Shape...  1.6 us
  transfers between devices with their start and end apart: 4, of which 3 were waited for; matrix products, arithmetic and copies ran while one was open for 0% of the time, Pallas kernels for 20%

commit v1 on v0

v1 whole, which is shorter than its diff:
```python
import functools

import jax
import jax.numpy as jnp
from jax import lax
from jax.experimental import pallas as pl
from jax.experimental.pallas import tpu as pltpu
from jax.sharding import PartitionSpec as P

HEAD_WIDTH = 128
QUERY_HEADS = 4
SCALE = HEAD_WIDTH ** (-0.5) * 1.4426950408889634
NEVER = -1e30
FLOOR = -5e29
SLOT_ROWS = 16
REACH = 2
VMEM_LIMIT = 32 * 1024 * 1024
VMEM_SMALL = 8 * 1024 * 1024

ANY = pl.BlockSpec(memory_space=pl.ANY)
SMEM = pl.BlockSpec(memory_space=pltpu.SMEM)
VMEM = pl.BlockSpec(memory_space=pltpu.VMEM)


def shifted(value, axis):
    count = lax.axis_size(axis)
    return lax.ppermute(value, axis, [(source, source + 1) for source in range(count - 1)])


def pack_kv_kernel(cap, targets, slots, keys, values, send, counts, slot_of):
    packs = send.shape[0]
    blocks = targets.shape[1]
    size = keys.shape[1] // blocks
    half = cap * size
    for t in range(packs):
        counts[t] = 0
    for j in range(blocks):
        t = targets[0, j]
        rank = counts[t]
        counts[t] = rank + 1
        slot_of[t * cap + rank] = lax.rem(slots[0, j], blocks)
        rows = slice(j * size, (j + 1) * size)
        to = pl.multiple_of(rank * size, size)
        send[t, pl.ds(to, size), :] = keys[0, rows, :]
        send[t, pl.ds(to + half, size), :] = values[0, rows, :]
    row = lax.broadcasted_iota(jnp.int32, (SLOT_ROWS, HEAD_WIDTH), 0)
    for t in range(packs):
        listed = jnp.zeros(row.shape, jnp.int32)
        for i in range(cap):
            listed = jnp.where(row == i, slot_of[t * cap + i], listed)
        send[t, 2 * half:, :] = listed.astype(jnp.float32).astype(jnp.bfloat16)


def pack_q_kernel(cap, targets, lengths, tiles, queries, send, bias, block_of, counts):
    packs = send.shape[0]
    blocks = targets.shape[1]
    tokens = queries.shape[1]
    size = tokens // blocks
    place = lax.axis_index("ctx")
    for t in range(packs):
        counts[t] = 0
    for j in range(blocks):
        t = targets[0, j]
        rank = counts[t]
        counts[t] = rank + 1
        to = pl.multiple_of(rank * size, size)
        send[t, pl.ds(to, size), :] = queries[0, j * size:(j + 1) * size, :]

    block = lax.broadcasted_iota(jnp.int32, (tokens, HEAD_WIDTH), 1)
    of_key = lax.broadcasted_iota(jnp.int32, (tokens, HEAD_WIDTH), 0) // size
    block_of[...] = (block == of_key).astype(jnp.float32).astype(jnp.bfloat16)
    query_block = place * blocks + lax.broadcasted_iota(jnp.int32, (blocks, 1), 0)
    listed_tiles = tiles[0].astype(jnp.float32).astype(jnp.bfloat16)
    for offset in range(bias.shape[0]):
        low = (place - offset) * blocks
        key_block = low + lax.broadcasted_iota(jnp.int32, (1, HEAD_WIDTH), 1)
        key_doc = jnp.zeros((1, HEAD_WIDTH), jnp.int32)
        query_doc = jnp.zeros((blocks, 1), jnp.int32)
        end = jnp.int32(0)
        for j in range(lengths.shape[1]):
            end = end + lengths[0, j]
            key_doc = key_doc + (key_block >= end).astype(jnp.int32)
            query_doc = query_doc + (query_block >= end).astype(jnp.int32)
        spread = lax.broadcasted_iota(jnp.int32, (tiles.shape[2], HEAD_WIDTH), 0) == key_block
        listed = jnp.dot(
            listed_tiles, spread.astype(jnp.float32).astype(jnp.bfloat16),
            preferred_element_type=jnp.float32,
        )
        allowed = (query_doc == key_doc) & (key_block <= query_block) & (key_block >= 0)
        allowed = allowed & ((listed > 0.5) | (key_block == query_block))
        bias[offset] = jnp.where(allowed, 0.0, NEVER)


def place_kernel(cap, received, keys, values, order):
    packs = received.shape[0]
    size = keys.shape[0] // (packs * cap)
    half = cap * size
    for s in range(packs):
        listed = received[s, 2 * half:, :].astype(jnp.float32).astype(jnp.int32)
        for i in range(cap):
            slot = listed[i, 0]
            order[0, slot] = s * cap + i
            rows = pl.ds(pl.multiple_of(slot * size, size), size)
            keys[rows, :] = received[s, i * size:(i + 1) * size, :]
            values[rows, :] = received[s, half + i * size:half + (i + 1) * size, :]


def first_document(lengths, position):
    start, end = jnp.int32(0), jnp.int32(0)
    total = jnp.int32(0)
    for j in range(lengths.shape[1]):
        after = total + lengths[0, j]
        inside = (total <= position) & (position < after)
        start = jnp.where(inside, total, start)
        end = jnp.where(inside, after, end)
        total = after
    return start, end


def reach_of(lengths, place, offset, blocks):
    start, end = first_document(lengths, place * blocks)
    low = (place - offset) * blocks
    rows = jnp.where(start < low + blocks, jnp.minimum(end - place * blocks, blocks), 0)
    return jnp.where(low >= 0, rows, 0), jnp.maximum(start - low, 0)


def beside_ones(values):
    return jnp.concatenate([values, jnp.ones(values.shape, values.dtype)], axis=1)


def score(received, order, bias, i, keys, block_of, size):
    source = pl.ds(pl.multiple_of(order[0, i] * size, size), size)
    barred = jnp.broadcast_to(bias[pl.ds(i, 1), :], (QUERY_HEADS * size, HEAD_WIDTH))
    rows = jnp.concatenate(
        [heads_as_rows(received[source, :]), barred.astype(jnp.bfloat16)], axis=1
    )
    return lax.dot_general(
        rows, jnp.concatenate([keys, block_of], axis=1), (((1,), (1,)), ((), ())), preferred_element_type=jnp.float32
    )


def heads_as_rows(block):
    return jnp.concatenate(
        [block[:, h * HEAD_WIDTH:(h + 1) * HEAD_WIDTH] for h in range(QUERY_HEADS)], axis=0
    )


def heads_as_columns(rows, size):
    return jnp.concatenate(
        [rows[h * size:(h + 1) * size] for h in range(QUERY_HEADS)], axis=1
    )


def own_kernel(first, last, order, bias_in, block_of, received, keys, values, *refs):
    out, state_o, state_l, stage, sem = refs[-5:]
    bias = bias_in.at[0]
    blocks = bias.shape[0]
    tokens = keys.shape[0]
    size = tokens // blocks
    group = QUERY_HEADS * size
    row = lax.rem(lax.broadcasted_iota(jnp.int32, (group, 2 * size), 0), size)
    lane = lax.broadcasted_iota(jnp.int32, (group, 2 * size), 1)

    def start(i):
        width = (i // 2 + 1) * 2 * size
        return score(received, order, bias, i, keys[:width, :], block_of[:width, :], size)

    copies = []
    scores = start(first)
    for i in range(first, last):
        ahead = start(i + 1) if i + 1 < last else None
        rows = slice(i * size, (i + 1) * size)
        span = slice(i * group, (i + 1) * group)
        width = scores.shape[1]
        edge = width - 2 * size
        tail = jnp.where(lane - (i % 2) * size > row, NEVER, scores[:, edge:])
        scores = jnp.concatenate([scores[:, :edge], tail], axis=1) if edge else tail
        top = jnp.max(scores, axis=1, keepdims=True) * SCALE
        weights = jnp.exp2(scores * SCALE - top).astype(jnp.bfloat16)
        sums = jnp.dot(weights, beside_ones(values[:width, :]), preferred_element_type=jnp.float32)
        denominator = sums[:, HEAD_WIDTH:]
        result = sums[:, :HEAD_WIDTH] / denominator
        stage[rows, :] = heads_as_columns(result, size).astype(jnp.bfloat16)
        state_o[span, :] = result
        state_l[span, :] = top + jnp.log2(denominator)
        copy = pltpu.make_async_copy(stage.at[rows], out.at[0, rows], sem.at[i])
        copy.start()
        copies.append(copy)
        scores = ahead
    for copy in copies:
        copy.wait()


def hop_kernel(
    offset, order, lengths, bias_in, block_of, received, keys, values,
    out_in, state_o_in, state_l_in,
    out, state_o, state_l,
    stage, sem,
):
    place = lax.axis_index("ctx")
    bias = bias_in.at[offset]
    blocks = bias.shape[0]
    tokens = keys.shape[0]
    size = tokens // blocks
    group = QUERY_HEADS * size
    reads, first = reach_of(lengths, place, offset, blocks)

    @pl.when(reads > 0)
    def _():
        def over(low, together):
            def start(i):
                return score(received, order, bias, i, keys[low:, :], block_of[low:, :], size)

            def end(i, scores):
                span = pl.ds(pl.multiple_of(i * group, group), group)
                top = jnp.maximum(jnp.max(scores, axis=1, keepdims=True), FLOOR) * SCALE
                weights = jnp.exp2(scores * SCALE - top).astype(jnp.bfloat16)
                sums = jnp.dot(weights, beside_ones(values[low:, :]), preferred_element_type=jnp.float32)
                before = state_l_in[span, :]
                most = jnp.maximum(before, top)
                old = jnp.exp2(before - most)
                new = jnp.exp2(top - most)
                denominator = old + new * sums[:, HEAD_WIDTH:]
                result = (
                    old * state_o_in[span, :] + new * sums[:, :HEAD_WIDTH]
                ) / denominator
                rows = pl.ds(pl.multiple_of(i * size, size), size)
                stage[rows, :] = heads_as_columns(result, size).astype(jnp.bfloat16)
                if offset == 1:
                    state_o[span, :] = result
                    state_l[span, :] = most + jnp.log2(denominator)

            def step(n, carry):
                i = n * together
                scores = start(i)
                for u in range(together):
                    ahead = start(i + u + 1) if u + 1 < together else None
                    end(i + u, scores)
                    scores = ahead
                rows = pl.ds(pl.multiple_of(i * size, size), together * size)
                pltpu.make_async_copy(stage.at[rows], out.at[0, rows], sem).start()
                return carry

            def finish(n, carry):
                rows = pl.ds(pl.multiple_of(n * together * size, size), together * size)
                pltpu.make_async_copy(stage.at[rows], out.at[0, rows], sem).wait()
                return carry

            steps = pl.cdiv(reads, together)
            lax.fori_loop(0, steps, step, 0)
            lax.fori_loop(0, steps, finish, 0)

        part = first // (blocks // 4)
        for n in range(4):
            pl.when(part == n)(functools.partial(over, n * (tokens // 4), 4))


def per_device(queries, keys, values, dest_replica, dest_slot, doc_lengths, tile_mask):
    tokens = queries.shape[1]
    width = queries.shape[2]
    blocks = dest_replica.shape[1]
    size = tokens // blocks
    packs = lax.axis_size("dp")
    cap = blocks // packs
    bf16, f32 = jnp.bfloat16, jnp.float32
    rows = tokens * QUERY_HEADS
    params = pltpu.CompilerParams(vmem_limit_bytes=VMEM_LIMIT)
    small = pltpu.CompilerParams(vmem_limit_bytes=VMEM_SMALL)

    def cost(flops, moved):
        return pl.CostEstimate(flops=flops, bytes_accessed=moved, transcendentals=0)

    def route(sent):
        return lax.all_to_all(sent, "dp", split_axis=0, concat_axis=0, tiled=True)

    dma = pltpu.SemaphoreType.DMA
    counts = pltpu.SMEM((packs,), jnp.int32)
    kv_send = pl.pallas_call(
        functools.partial(pack_kv_kernel, cap),
        out_shape=jax.ShapeDtypeStruct((packs, 2 * cap * size + SLOT_ROWS, HEAD_WIDTH), bf16),
        in_specs=[SMEM, SMEM, VMEM, VMEM],
        out_specs=VMEM,
        scratch_shapes=[counts, pltpu.SMEM((blocks,), jnp.int32)],
        cost_estimate=cost(0, 4 * tokens * HEAD_WIDTH * 2),
        name="pack_kv",
    )(dest_replica, dest_slot, keys, values)
    kv_recv = route(kv_send)
    q_send, bias, block_of = pl.pallas_call(
        functools.partial(pack_q_kernel, cap),
        out_shape=(
            jax.ShapeDtypeStruct((packs, cap * size, width), bf16),
            jax.ShapeDtypeStruct((REACH + 1, blocks, HEAD_WIDTH), f32),
            jax.ShapeDtypeStruct((tokens, HEAD_WIDTH), bf16),
        ),
        in_specs=[SMEM, SMEM, VMEM, VMEM],
        out_specs=(VMEM, VMEM, VMEM),
        scratch_shapes=[counts],
        compiler_params=small,
        cost_estimate=cost(0, 2 * tokens * width * 2),
        name="pack_q",
    )(dest_replica, doc_lengths, tile_mask, queries)
    q_recv = route(q_send).reshape(tokens, width)
    moving_k, moving_v, order = pl.pallas_call(
        functools.partial(place_kernel, cap),
        out_shape=(
            jax.ShapeDtypeStruct((tokens, HEAD_WIDTH), bf16),
            jax.ShapeDtypeStruct((tokens, HEAD_WIDTH), bf16),
            jax.ShapeDtypeStruct((1, blocks), jnp.int32),
        ),
        in_specs=[VMEM],
        out_specs=(VMEM, VMEM, SMEM),
        compiler_params=small,
        cost_estimate=cost(0, 4 * tokens * HEAD_WIDTH * 2),
        name="place_kv",
    )(kv_recv)

    state_shapes = (
        jax.ShapeDtypeStruct((1, tokens, width), bf16),
        jax.ShapeDtypeStruct((rows, HEAD_WIDTH), f32),
        jax.ShapeDtypeStruct((rows, HEAD_WIDTH), f32),
    )
    stage = pltpu.VMEM((tokens, width), bf16)

    def attend_own(first, last, *state):
        return pl.pallas_call(
            functools.partial(own_kernel, first, last),
            out_shape=state_shapes,
            in_specs=[SMEM] + [VMEM] * 5 + [ANY, VMEM, VMEM][:len(state)],
            out_specs=(ANY, VMEM, VMEM),
            scratch_shapes=[stage, dma((blocks,))],
            input_output_aliases={6 + n: n for n in range(len(state))},
            compiler_params=params,
            cost_estimate=cost(2 * rows * tokens * HEAD_WIDTH, 8 * tokens * width),
            name=f"attend_own_{first}",
        )(order, bias, block_of, q_recv, moving_k, moving_v, *state)

    def attend_back(offset, keys, values, *state):
        return pl.pallas_call(
            functools.partial(hop_kernel, offset),
            out_shape=state_shapes,
            in_specs=[SMEM, SMEM] + [VMEM] * 5 + [ANY, VMEM, VMEM],
            out_specs=(ANY, VMEM, VMEM),
            scratch_shapes=[stage, dma],
            input_output_aliases={7: 0, 8: 1, 9: 2},
            compiler_params=params,
            cost_estimate=cost(2 * 2 * rows * tokens * HEAD_WIDTH, 8 * tokens * width),
            name=f"attend_back_{offset}",
        )(order, doc_lengths, bias, block_of, q_recv, keys, values, *state)

    middle = blocks * 5 // 16 * 2
    back_k = shifted(moving_k, "ctx")
    back_v = shifted(moving_v, "ctx")
    state = attend_own(0, middle)
    far_v, *state = lax.optimization_barrier((back_v, *state))
    far_k = shifted(back_k, "ctx")
    far_v = shifted(far_v, "ctx")
    state = attend_own(middle, blocks, *state)
    state = attend_back(1, back_k, back_v, *state)
    state = attend_back(2, far_k, far_v, *state)
    return state[0]


def solution(mesh):
    return jax.shard_map(
        per_device,
        mesh=mesh,
        in_specs=(
            P("dp", "ctx", None),
            P("dp", "ctx", None),
            P("dp", "ctx", None),
            P("dp", "ctx"),
            P("dp", "ctx"),
            P("dp", None),
            P("dp", "ctx", None),
        ),
        out_specs=P("dp", "ctx", None),
        check_vma=False,
    )
```

time: 60.8 us -> 55.7 us (0.916)
  the two profiles are of different devices: /device:TPU:27 before, /device:TPU:20 now
where the time goes in v1:
time: 55.7 us; the launch traced here: 56.4 us
  Pallas kernels  23.4 us (42%)
  starting transfers between devices  20.4 us (37%)
  waiting for transfers between devices  12.5 us (22%)
    pallas_call x2, Pallas kernels, attend_back(): pl.pallas_call(functools.partial(hop_kernel, offset), out_shape=state_sha...  12.1 us
    ppermute x4, starting transfers between devices, shifted(): lax.ppermute(value, axis, [(source, source + 1) for source in range(count...  11.2 us
    all_to_all x2, starting transfers between devices, route(): return lax.all_to_all(sent, 'dp', split_axis=0, concat_axis=0, tiled=True)  9.17 us
    all_to_all x2, waiting for transfers between devices, route(): return lax.all_to_all(sent, 'dp', split_axis=0, concat_axis=0, tiled=True)  6.89 us
    pallas_call x2, Pallas kernels, attend_own(): pl.pallas_call(functools.partial(own_kernel, first, last), out_shape=stat...  6.81 us
    ppermute x4, waiting for transfers between devices, shifted(): lax.ppermute(value, axis, [(source, source + 1) for source in range(count...  5.63 us
    pallas_call x1, Pallas kernels, per_device(): pl.pallas_call(functools.partial(pack_kv_kernel, cap), out_shape=jax.Shap...  2.09 us
    pallas_call x1, Pallas kernels, per_device(): pl.pallas_call(functools.partial(pack_q_kernel, cap), out_shape=(jax.Shap...  1.72 us
  transfers between devices with their start and end apart: 6, of which 2 were waited for; matrix products, arithmetic and copies ran while one was open for 0% of the time, Pallas kernels for 30%

profile of v1, /device:TPU:20, one launch (start us, length us, event | category | flops | bytes accessed | tf_op | source)
XLA Modules:
  0.0 56.4 jit_solution(11612220154862289877)
XLA Ops:
  0.0 0.0 copy-start.2
  0.0 0.0 copy-start.3
  0.0 0.0 copy-start.1
  0.0 0.0 copy-start
  0.0 2.1 %pack_kv.1 = bf16[8,272,128]{2,1,0:T(8,128)(2,1)} custom-call(s32[1,16]{1,0:T(1,128)} %targets.3, s32[1,16]{1,0:T(1,128)} %slots.1, bf16[1,1024,128]{2,1,0:T(8,128)(2,1)} %keys.1, bf16[1,1024,128]{2,1,0:T(8,128)(2,1)} %values.1), custom_call_target="tpu_custom_call" | custom-call | bytes 1048576 | tf_op jit(solution)/shard_map/pack_kv/pallas_call | solution.py:278
  2.1 4.2 %all-to-all-start = ((bf16[8,272,128]{2,1,0:T(8,128)(2,1)}), bf16[8,272,128]{2,1,0:T(8,128)(2,1)S(1)}, u32[]{:S(2)}, u32[]{:S(2)}) async-start(bf16[8,272,128]{2,1,0:T(8,128)(2,1)} %pack_kv.1), calls=%async_computation | async-start | bytes 1114112 | tf_op jit(solution)/shard_map/all_to_all | solution.py:274
  6.3 0.0 copy-done.2
  6.3 0.0 copy-done.3
  6.3 0.0 copy-done.1
  6.4 0.0 copy-done
  6.4 1.7 %pack_q.1 = (bf16[8,128,512]{2,1,0:T(8,128)(2,1)}, f32[3,16,128]{2,1,0:T(8,128)S(1)}, bf16[1024,128]{1,0:T(8,128)(2,1)S(1)}) custom-call(s32[1,16]{1,0:T(1,128)S(1)} %copy-done.2, s32[1,16]{1,0:T(1,128)S(1)} %copy-done.3, s32[1,16,64]{2,1,0:T(8,128)S(1)} %copy-done.1, bf16[1,1024,512]{2,1,0:T(8,128)(2,1)S(1)} %copy-done), custom_call_target="tpu_custom_call" | custom-call | bytes 2097152 | tf_op jit(solution)/shard_map/pack_q/pallas_call | solution.py:288
  8.1 6.9 %all-to-all-done.received = bf16[8,272,128]{2,1,0:T(8,128)(2,1)S(1)} async-done(((bf16[8,272,128]{2,1,0:T(8,128)(2,1)}), bf16[8,272,128]{2,1,0:T(8,128)(2,1)S(1)}, u32[]{:S(2)}, u32[]{:S(2)}) %all-to-all-start) | async-done | bytes 557088 | tf_op jit(solution)/shard_map/all_to_all | solution.py:274
  15.0 4.9 %all-to-all-start.1 = ((bf16[8,128,512]{2,1,0:T(8,128)(2,1)}), bf16[8,128,512]{2,1,0:T(8,128)(2,1)S(1)}, u32[]{:S(2)}, u32[]{:S(2)}) async-start(bf16[8,128,512]{2,1,0:T(8,128)(2,1)} %get-tuple-element.28), calls=%async_computation.1 | async-start | bytes 2097152 | tf_op jit(solution)/shard_map/all_to_all | solution.py:274
  19.9 0.7 %place_kv.1 = (bf16[1024,128]{1,0:T(8,128)(2,1)S(1)}, bf16[1024,128]{1,0:T(8,128)(2,1)S(1)}, s32[1,16]{1,0:T(1,128)S(1)}) custom-call(bf16[8,272,128]{2,1,0:T(8,128)(2,1)S(1)} %all-to-all-done.received), custom_call_target="tpu_custom_call" | custom-call | bytes 1048576 | tf_op jit(solution)/shard_map/place_kv/pallas_call | solution.py:303
  20.6 3.5 %collective-permute-start = (bf16[1024,128]{1,0:T(8,128)(2,1)S(1)}, bf16[1024,128]{1,0:T(8,128)(2,1)S(1)}, u32[]{:S(2)}, u32[]{:S(2)}) collective-permute-start(bf16[1024,128]{1,0:T(8,128)(2,1)S(1)} %get-tuple-element.29.keys), channel_id=1, source_target_pairs={{0,1},{1,2},{2,3},{4,5},{5,6},{6,7},{8,9},{9,10},{10,11},{12,13},{... | collective-permute-start | bytes 786440 | tf_op jit(solution)/shard_map/ppermute | solution.py:27
  24.1 1.9 %collective-permute-start.2 = (bf16[1024,128]{1,0:T(8,128)(2,1)S(1)}, bf16[1024,128]{1,0:T(8,128)(2,1)S(1)}, u32[]{:S(2)}, u32[]{:S(2)}) collective-permute-start(bf16[1024,128]{1,0:T(8,128)(2,1)S(1)} %get-tuple-element.30.values), channel_id=1, source_target_pairs={{0,1},{1,2},{2,3},{4,5},{5,6},{6,7},{8,9},{9,10},{10,11},{12,13},{... | collective-permute-start | bytes 786440 | tf_op jit(solution)/shard_map/ppermute | solution.py:27
  26.0 5.6 %collective-permute-done.keys = bf16[1024,128]{1,0:T(8,128)(2,1)S(1)} collective-permute-done((bf16[1024,128]{1,0:T(8,128)(2,1)S(1)}, bf16[1024,128]{1,0:T(8,128)(2,1)S(1)}, u32[]{:S(2)}, u32[]{:S(2)}) %collective-permute-start) | collective-permute-done | bytes 262176 | tf_op jit(solution)/shard_map/ppermute | solution.py:27
  31.6 3.5 %collective-permute-start.1 = (bf16[1024,128]{1,0:T(8,128)(2,1)S(1)}, bf16[1024,128]{1,0:T(8,128)(2,1)S(1)}, u32[]{:S(2)}, u32[]{:S(2)}) collective-permute-start(bf16[1024,128]{1,0:T(8,128)(2,1)S(1)} %collective-permute-done.keys), channel_id=1, source_target_pairs={{0,1},{1,2},{2,3},{4,5},{5,6},{6,7},{8,9},{9,10},{10,11},{12,13},{... | collective-permute-start | bytes 786440 | tf_op jit(solution)/shard_map/ppermute | solution.py:27
  35.1 0.0 all-to-all-done.1
  35.1 3.3 %attend_own_0.1 = (bf16[1,1024,512]{2,1,0:T(8,128)(2,1)}, f32[4096,128]{1,0:T(8,128)S(1)}, f32[4096,128]{1,0:T(8,128)S(1)}) custom-call(s32[1,16]{1,0:T(1,128)S(1)} %get-tuple-element.25.order, f32[3,16,128]{2,1,0:T(8,128)S(1)} %get-tuple-element.26.bias_in, bf16[1024,128]{1,0:T(8,128)(2,1)S(1)} %get-tuple-element.27.block_of, ...), custom_call_target="tpu_custom_call" | custom-call | flops 1073741824 | bytes 4194304 | tf_op jit(solution)/shard_map/attend_own_0/pallas_call | solution.py:325
  38.4 0.0 collective-permute-done.2.values
  38.4 2.3 %collective-permute-start.3 = (bf16[1024,128]{1,0:T(8,128)(2,1)S(1)}, bf16[1024,128]{1,0:T(8,128)(2,1)S(1)}, u32[]{:S(2)}, u32[]{:S(2)}) collective-permute-start(bf16[1024,128]{1,0:T(8,128)(2,1)S(1)} %collective-permute-done.2.values), channel_id=1, source_target_pairs={{0,1},{1,2},{2,3},{4,5},{5,6},{6,7},{8,9},{9,10},{10,11},{12,13},{... | collective-permute-start | bytes 786440 | tf_op jit(solution)/shard_map/ppermute | solution.py:27
  40.7 3.5 %attend_own_10.1 = (bf16[1,1024,512]{2,1,0:T(8,128)(2,1)}, f32[4096,128]{1,0:T(8,128)S(1)}, f32[4096,128]{1,0:T(8,128)S(1)}) custom-call(s32[1,16]{1,0:T(1,128)S(1)} %get-tuple-element.25.order, f32[3,16,128]{2,1,0:T(8,128)S(1)} %get-tuple-element.26.bias_in, ...), custom_call_target="tpu_custom_call", output_to_operand_aliasing={{0}: (6, {}), {1}: (7, {}), {2}: (8, {})} | custom-call | flops 1073741824 | bytes 4194304 | tf_op jit(solution)/shard_map/attend_own_10/pallas_call | solution.py:325
  44.3 7.9 %attend_back_1.1 = (bf16[1,1024,512]{2,1,0:T(8,128)(2,1)}, f32[4096,128]{1,0:T(8,128)S(1)}, f32[4096,128]{1,0:T(8,128)S(1)}) custom-call(s32[1,16]{1,0:T(1,128)S(1)} %get-tuple-element.25.order, s32[1,16]{1,0:T(1,128)S(1)} %copy-done.3, f32[3,16,128]{2,1,0:T(8,128)S(1)} %get-tuple-element.26.bias_in, ...), custom_call_target="tpu_custom_call", output_to_operand_aliasing={{0}: (7, {}), {1}: (8, {}), {2}: (9, {})} | custom-call | flops 2147483648 | bytes 4194304 | tf_op jit(solution)/shard_map/attend_back_1/pallas_call | solution.py:338
  52.2 0.0 collective-permute-done.1.keys
  52.2 0.0 collective-permute-done.3.values
  52.2 4.2 %attend_back_2.1 = (bf16[1,1024,512]{2,1,0:T(8,128)(2,1)}, f32[4096,128]{1,0:T(8,128)S(1)}, f32[4096,128]{1,0:T(8,128)S(1)}) custom-call(s32[1,16]{1,0:T(1,128)S(1)} %get-tuple-element.25.order, s32[1,16]{1,0:T(1,128)S(1)} %copy-done.3, f32[3,16,128]{2,1,0:T(8,128)S(1)} %get-tuple-element.26.bias_in, ...), custom_call_target="tpu_custom_call", output_to_operand_aliasing={{0}: (7, {}), {1}: (8, {}), {2}: (9, {})} | custom-call | flops 2147483648 | bytes 4194304 | tf_op jit(solution)/shard_map/attend_back_2/pallas_call | solution.py:338
Async XLA Ops:
  0.0 6.3 %copy-start.2 = (s32[1,16]{1,0:T(1,128)S(1)}, s32[1,16]{1,0:T(1,128)}, u32[]{:S(2)}) copy-start(s32[1,16]{1,0:T(1,128)} %targets.3) | copy-start | bytes 196
  0.0 6.3 %copy-start.3 = (s32[1,16]{1,0:T(1,128)S(1)}, s32[1,16]{1,0:T(1,128)}, u32[]{:S(2)}) copy-start(s32[1,16]{1,0:T(1,128)} %lengths.5) | copy-start | bytes 196
  0.0 6.3 %copy-start.1 = (s32[1,16,64]{2,1,0:T(8,128)S(1)}, s32[1,16,64]{2,1,0:T(8,128)}, u32[]{:S(2)}) copy-start(s32[1,16,64]{2,1,0:T(8,128)} %tiles.1) | copy-start | bytes 12292
  0.0 6.3 %copy-start = (bf16[1,1024,512]{2,1,0:T(8,128)(2,1)S(1)}, bf16[1,1024,512]{2,1,0:T(8,128)(2,1)}, u32[]{:S(2)}) copy-start(bf16[1,1024,512]{2,1,0:T(8,128)(2,1)} %queries.1) | copy-start | bytes 3145732
  2.1 12.9 %all-to-all-start = ((bf16[8,272,128]{2,1,0:T(8,128)(2,1)}), bf16[8,272,128]{2,1,0:T(8,128)(2,1)S(1)}, u32[]{:S(2)}, u32[]{:S(2)}) async-start(bf16[8,272,128]{2,1,0:T(8,128)(2,1)} %pack_kv.1), calls=%async_computation | async-start | bytes 1114112 | tf_op jit(solution)/shard_map/all_to_all | solution.py:274
  15.0 20.1 %all-to-all-start.1 = ((bf16[8,128,512]{2,1,0:T(8,128)(2,1)}), bf16[8,128,512]{2,1,0:T(8,128)(2,1)S(1)}, u32[]{:S(2)}, u32[]{:S(2)}) async-start(bf16[8,128,512]{2,1,0:T(8,128)(2,1)} %get-tuple-element.28), calls=%async_computation.1 | async-start | bytes 2097152 | tf_op jit(solution)/shard_map/all_to_all | solution.py:274
  20.6 11.0 %collective-permute-start = (bf16[1024,128]{1,0:T(8,128)(2,1)S(1)}, bf16[1024,128]{1,0:T(8,128)(2,1)S(1)}, u32[]{:S(2)}, u32[]{:S(2)}) collective-permute-start(bf16[1024,128]{1,0:T(8,128)(2,1)S(1)} %get-tuple-element.29.keys), channel_id=1, source_target_pairs={{0,1},{1,2},{2,3},{4,5},{5,6},{6,7},{8,9},{9,10},{10,11},{12,13},{... | collective-permute-start | bytes 786440 | tf_op jit(solution)/shard_map/ppermute | solution.py:27
  24.1 14.3 %collective-permute-start.2 = (bf16[1024,128]{1,0:T(8,128)(2,1)S(1)}, bf16[1024,128]{1,0:T(8,128)(2,1)S(1)}, u32[]{:S(2)}, u32[]{:S(2)}) collective-permute-start(bf16[1024,128]{1,0:T(8,128)(2,1)S(1)} %get-tuple-element.30.values), channel_id=1, source_target_pairs={{0,1},{1,2},{2,3},{4,5},{5,6},{6,7},{8,9},{9,10},{10,11},{12,13},{... | collective-permute-start | bytes 786440 | tf_op jit(solution)/shard_map/ppermute | solution.py:27
  31.6 20.6 %collective-permute-start.1 = (bf16[1024,128]{1,0:T(8,128)(2,1)S(1)}, bf16[1024,128]{1,0:T(8,128)(2,1)S(1)}, u32[]{:S(2)}, u32[]{:S(2)}) collective-permute-start(bf16[1024,128]{1,0:T(8,128)(2,1)S(1)} %collective-permute-done.keys), channel_id=1, source_target_pairs={{0,1},{1,2},{2,3},{4,5},{5,6},{6,7},{8,9},{9,10},{10,11},{12,13},{... | collective-permute-start | bytes 786440 | tf_op jit(solution)/shard_map/ppermute | solution.py:27
  38.4 13.8 %collective-permute-start.3 = (bf16[1024,128]{1,0:T(8,128)(2,1)S(1)}, bf16[1024,128]{1,0:T(8,128)(2,1)S(1)}, u32[]{:S(2)}, u32[]{:S(2)}) collective-permute-start(bf16[1024,128]{1,0:T(8,128)(2,1)S(1)} %collective-permute-done.2.values), channel_id=1, source_target_pairs={{0,1},{1,2},{2,3},{4,5},{5,6},{6,7},{8,9},{9,10},{10,11},{12,13},{... | collective-permute-start | bytes 786440 | tf_op jit(solution)/shard_map/ppermute | solution.py:27
